TPU v7x, 256 devices: a whole 4x4x8 slice. The times are simulated.
256 devices in a mesh: tm: 64 (over z, y, core), sub: 4 (over x).
Axes of the slice: x: 4, y: 4, z: 8, core: 2. Of those that a mesh axis runs over, the one named last changes fastest.
Arguments:
- transition: float32 [512, 256, 256], P(('tm', 'sub')), may hold values from -1 to 2
- precision: float32 [512, 256], P(('tm', 'sub')), may hold values from 4e-05 to 1.01
- info: float32 [512, 256, 128], P(('tm', 'sub')), may hold values from -2 to 2
Outputs:
- smoothed: float32 [512, 256, 128], P(('tm', 'sub'))
All inputs are finite; a program needn't handle non-finite values.
Results may differ from a plain program's by a relative error of at most 0.0027.
Values sent between devices are 32-bit elements; how exact they have to be, the bound alone decides.
A program may use at most 128 MiB of HBM per device.

v0:
```python
import jax
import jax.numpy as jnp
from jax import lax
from jax.sharding import PartitionSpec as P

LEVELS = 8


HIGHEST = lax.Precision.HIGHEST


def from_behind(array, axis, by):
    size = lax.axis_size(axis)
    pairs = [(i, i + by) for i in range(size) if 0 <= i + by < size]
    return lax.ppermute(array, axis, pairs)


def multiply(left_side, right_side):
    return jnp.dot(left_side, right_side, precision=HIGHEST, preferred_element_type=jnp.float32)


def solve_with(factor, right_side):
    return jax.scipy.linalg.cho_solve((factor, True), right_side)


def scaled(system):
    diagonal, lower, upper, source = system
    return solve_with(jnp.linalg.cholesky(diagonal), jnp.concatenate([lower, upper, source], 1))


def reduce_level(system, from_left, from_right, at_last):
    diagonal, lower, upper, source = system
    states = diagonal.shape[0]
    if at_last:
        left_part = multiply(lower, from_left[:, states:])
        right_part = multiply(
            upper, jnp.concatenate([from_right[:, :states], from_right[:, 2 * states :]], 1)
        )
        zeros_block = jnp.zeros_like(lower)
        return (
            diagonal - left_part[:, :states] - right_part[:, :states],
            zeros_block,
            zeros_block,
            source - left_part[:, states:] - right_part[:, states:],
        )
    left_part = multiply(lower, from_left)
    right_part = multiply(upper, from_right)
    return (
        diagonal - left_part[:, states : 2 * states] - right_part[:, :states],
        -left_part[:, :states],
        -right_part[:, states : 2 * states],
        source - left_part[:, 2 * states :] - right_part[:, 2 * states :],
    )


def shards(transition, precision, info):
    local_steps, states, columns = info.shape
    interior_steps = local_steps - 1
    total_cols = 2 * states + columns
    sub_size = lax.axis_size("sub")
    device_count = lax.axis_size("tm") * sub_size
    device = lax.axis_index("tm") * sub_size + lax.axis_index("sub")
    identity = jnp.eye(states, dtype=jnp.float32)
    following = from_behind(transition[0], ("tm", "sub"), -1)
    successors = jnp.concatenate([transition[1:], following[None]], 0)
    diagonal = (
        identity[None]
        + identity[None] * precision[:, None, :]
        + jnp.einsum(
            "tji,tjk->tik",
            successors,
            successors,
            precision=HIGHEST,
            preferred_element_type=jnp.float32,
        )
    )
    first_coupling = transition[0] * (device > 0).astype(jnp.float32)
    right_sides = jnp.zeros((interior_steps, states, total_cols), jnp.float32)
    right_sides = right_sides.at[0, :, :states].set(-first_coupling)
    right_sides = right_sides.at[interior_steps - 1, :, states : 2 * states].add(
        -transition[local_steps - 1].T
    )
    right_sides = right_sides.at[:, :, 2 * states :].set(info[:interior_steps])
    schur_block = diagonal[0]
    remainder = right_sides[0]
    factors = [jnp.linalg.cholesky(schur_block)]
    remainders = [remainder]
    solutions = [None] * interior_steps
    later_block = solve_with(factors[interior_steps - 1], remainders[interior_steps - 1])
    solutions[interior_steps - 1] = later_block
    own_terms = multiply(transition[local_steps - 1], solutions[interior_steps - 1])
    outgoing = multiply(first_coupling.T, solutions[0])
    incoming = from_behind(outgoing, ("tm", "sub"), -1)
    system = (
        diagonal[local_steps - 1] + own_terms[:, states : 2 * states] + incoming[:, :states],
        own_terms[:, :states],
        incoming[:, states : 2 * states],
        info[local_steps - 1] + own_terms[:, 2 * states :] + incoming[:, 2 * states :],
    )
    for depth_level in range(LEVELS):
        stride = 2**depth_level
        at_last = 2 * stride >= device_count
        sending = scaled(system)
        from_left = from_behind(sending, ("tm", "sub"), stride)
        from_right = from_behind(sending, ("tm", "sub"), -stride)
        system = reduce_level(system, from_left, from_right, at_last)
    separator = solve_with(jnp.linalg.cholesky(system[0]), system[3])
    previous = from_behind(separator, ("tm", "sub"), 1)
    neighbours = jnp.concatenate([previous, separator], 0)
    stacked = jnp.stack(solutions)
    interior = stacked[:, :, 2 * states :] - jnp.einsum(
        "kij,jr->kir",
        stacked[:, :, : 2 * states],
        neighbours,
        precision=HIGHEST,
        preferred_element_type=jnp.float32,
    )
    return jnp.concatenate([interior, separator[None]], 0)


def solution(mesh):
    placed = (P(("tm", "sub"), None, None), P(("tm", "sub"), None), P(("tm", "sub"), None, None))
    return jax.shard_map(
        shards, mesh=mesh, in_specs=placed, out_specs=P(("tm", "sub"), None, None), check_vma=False
    )
```

profile of v0, /device:TPU:1, one launch (start us, length us, event | category | flops | bytes accessed | tf_op | source)
XLA Modules:
  0.0 962.6 jit_solution(11515955284774573604)
XLA Ops:
  1.1 5.8 collective-permute-start
  15.7 11.7 %cholesky.466 = f32[128,128]{1,0:T(8,128)S(1)} custom-call(f32[128,128]{1,0:T(8,128)S(1)} %cholesky.802), custom_call_target="Cholesky" | custom-call | tf_op jit(solution)/shard_map/jit(cholesky)/cholesky | solution.py:86
  27.4 9.8 %custom-call.38 = f32[1,128,128]{1,2,0:T(8,128)S(1)} custom-call(f32[1,128,128]{2,1,0:T(8,128)S(1)} %get-tuple-element.291), custom_call_target="InvertDiagBlocksLowerTriangular" | custom-call | tf_op jit(solution)/shard_map/jit(cholesky)/cholesky | solution.py:86
  37.8 11.7 %cholesky.483 = f32[128,128]{1,0:T(8,128)S(1)} custom-call(f32[128,128]{1,0:T(8,128)S(1)} %convolution_subtract_fusion.28), custom_call_target="Cholesky" | custom-call | tf_op jit(solution)/shard_map/jit(cholesky)/cholesky | solution.py:86
  55.3 20.1 %custom-call.39 = f32[2,128,128]{1,2,0:T(8,128)S(1)} custom-call(f32[2,128,128]{2,1,0:T(8,128)S(1)} %get-tuple-element.107), custom_call_target="InvertDiagBlocksLowerTriangular" | custom-call | tf_op jit(solution)/shard_map/jit(_cho_solve)/triangular_solve | solution.py:23
  86.4 12.9 %collective-permute-done.1 = f32[256,640]{0,1:T(8,128)S(1)} collective-permute-done((f32[256,640]{0,1:T(8,128)}, f32[256,640]{0,1:T(8,128)S(1)}, u32[]{:S(2)}, u32[]{:S(2)}) %collective-permute-start.1) | collective-permute-done | bytes 655392 | tf_op jit(solution)/shard_map/ppermute | solution.py:15
  100.3 11.7 %cholesky.500 = f32[128,128]{1,0:T(8,128)S(1)} custom-call(f32[128,128]{1,0:T(8,128)S(1)} %cholesky.805), custom_call_target="Cholesky" | custom-call | tf_op jit(solution)/shard_map/jit(cholesky)/cholesky | solution.py:28
  112.1 9.8 %custom-call.40 = f32[1,128,128]{1,2,0:T(8,128)S(1)} custom-call(f32[1,128,128]{2,1,0:T(8,128)S(1)} %get-tuple-element.287), custom_call_target="InvertDiagBlocksLowerTriangular" | custom-call | tf_op jit(solution)/shard_map/jit(cholesky)/cholesky | solution.py:28
  122.4 11.7 %cholesky.517 = f32[128,128]{1,0:T(8,128)S(1)} custom-call(f32[128,128]{1,0:T(8,128)S(1)} %convolution_subtract_fusion.27), custom_call_target="Cholesky" | custom-call | tf_op jit(solution)/shard_map/jit(cholesky)/cholesky | solution.py:28
  136.7 16.1 %while.24 = (s32[]{:T(128)}, f32[256,256]{1,0:T(8,128)S(1)}, s32[2,2]{1,0:T(2,128)S(1)}, f32[2,128,128]{2,1,0:T(8,128)S(1)}, s32[]{:T(128)}) while((s32[]{:T(128)}, f32[256,256]{1,0:T(8,128)S(1)}, s32[2,2]{1,0:T(2,128)S(1)}, f32[2,128,128]{2,1,0:T(8,128)S(1)}, s32[]{:T(128)}) %tuple.241), condition=%wide.while_cond.3.clone, body=%wide.while_body.3.clone.sunk | while | flops 2 | bytes 131181 | solution.py:23
  152.8 20.3 %custom-call.41 = f32[2,128,128]{1,2,0:T(8,128)} custom-call(f32[2,128,128]{2,1,0:T(8,128)S(1)} %get-tuple-element.108), custom_call_target="InvertDiagBlocksLowerTriangular" | custom-call | tf_op jit(solution)/shard_map/jit(_cho_solve)/triangular_solve | solution.py:23
  180.8 4.9 collective-permute-start.3
  185.6 12.5 %collective-permute-done.2 = f32[256,640]{1,0:T(8,128)} collective-permute-done((f32[256,640]{1,0:T(8,128)}, f32[256,640]{1,0:T(8,128)}, u32[]{:S(2)}, u32[]{:S(2)}) %collective-permute-start.2) | collective-permute-done | bytes 655392 | tf_op jit(solution)/shard_map/ppermute | solution.py:15
  204.1 11.7 %cholesky.534 = f32[128,128]{1,0:T(8,128)S(1)} custom-call(f32[128,128]{1,0:T(8,128)S(1)} %cholesky.808), custom_call_target="Cholesky" | custom-call | tf_op jit(solution)/shard_map/jit(cholesky)/cholesky | solution.py:28
  215.9 9.8 %custom-call.42 = f32[1,128,128]{1,2,0:T(8,128)S(1)} custom-call(f32[1,128,128]{2,1,0:T(8,128)S(1)} %get-tuple-element.283), custom_call_target="InvertDiagBlocksLowerTriangular" | custom-call | tf_op jit(solution)/shard_map/jit(cholesky)/cholesky | solution.py:28
  226.2 12.1 %cholesky.551 = f32[128,128]{1,0:T(8,128)S(1)} custom-call(f32[128,128]{1,0:T(8,128)S(1)} %convolution_subtract_fusion.26), custom_call_target="Cholesky" | custom-call | tf_op jit(solution)/shard_map/jit(cholesky)/cholesky | solution.py:28
  241.1 4.3 while.25
  245.4 19.7 %custom-call.43 = f32[2,128,128]{1,2,0:T(8,128)S(1)} custom-call(f32[2,128,128]{2,1,0:T(8,128)S(1)} %get-tuple-element.109), custom_call_target="InvertDiagBlocksLowerTriangular" | custom-call | tf_op jit(solution)/shard_map/jit(_cho_solve)/triangular_solve | solution.py:23
  269.9 5.2 collective-permute-start.4
  277.0 19.6 %collective-permute-done.4 = f32[256,640]{1,0:T(8,128)S(1)} collective-permute-done((f32[256,640]{1,0:T(8,128)}, f32[256,640]{1,0:T(8,128)S(1)}, u32[]{:S(2)}, u32[]{:S(2)}) %collective-permute-start.4) | collective-permute-done | bytes 655392 | tf_op jit(solution)/shard_map/ppermute | solution.py:15
  298.2 6.5 collective-permute-done.5
  307.9 11.7 %cholesky.568 = f32[128,128]{1,0:T(8,128)S(1)} custom-call(f32[128,128]{1,0:T(8,128)S(1)} %cholesky.811), custom_call_target="Cholesky" | custom-call | tf_op jit(solution)/shard_map/jit(cholesky)/cholesky | solution.py:28
  319.7 9.8 %custom-call.44 = f32[1,128,128]{1,2,0:T(8,128)S(1)} custom-call(f32[1,128,128]{2,1,0:T(8,128)S(1)} %get-tuple-element.279), custom_call_target="InvertDiagBlocksLowerTriangular" | custom-call | tf_op jit(solution)/shard_map/jit(cholesky)/cholesky | solution.py:28
  330.0 11.9 %cholesky.585 = f32[128,128]{1,0:T(8,128)S(1)} custom-call(f32[128,128]{1,0:T(8,128)S(1)} %convolution_subtract_fusion.25), custom_call_target="Cholesky" | custom-call | tf_op jit(solution)/shard_map/jit(cholesky)/cholesky | solution.py:28
  344.8 4.3 while.26
  349.0 19.7 %custom-call.45 = f32[2,128,128]{1,2,0:T(8,128)S(1)} custom-call(f32[2,128,128]{2,1,0:T(8,128)S(1)} %get-tuple-element.110), custom_call_target="InvertDiagBlocksLowerTriangular" | custom-call | tf_op jit(solution)/shard_map/jit(_cho_solve)/triangular_solve | solution.py:23
  379.3 5.9 collective-permute-done.6
  392.9 11.7 %cholesky.602 = f32[128,128]{1,0:T(8,128)S(1)} custom-call(f32[128,128]{1,0:T(8,128)S(1)} %cholesky.814), custom_call_target="Cholesky" | custom-call | tf_op jit(solution)/shard_map/jit(cholesky)/cholesky | solution.py:28
  404.7 9.8 %custom-call.46 = f32[1,128,128]{1,2,0:T(8,128)S(1)} custom-call(f32[1,128,128]{2,1,0:T(8,128)S(1)} %get-tuple-element.275), custom_call_target="InvertDiagBlocksLowerTriangular" | custom-call | tf_op jit(solution)/shard_map/jit(cholesky)/cholesky | solution.py:28
  415.0 11.7 %cholesky.619 = f32[128,128]{1,0:T(8,128)S(1)} custom-call(f32[128,128]{1,0:T(8,128)S(1)} %convolution_subtract_fusion.24), custom_call_target="Cholesky" | custom-call | tf_op jit(solution)/shard_map/jit(cholesky)/cholesky | solution.py:28
  433.6 19.7 %custom-call.47 = f32[2,128,128]{1,2,0:T(8,128)S(1)} custom-call(f32[2,128,128]{2,1,0:T(8,128)S(1)} %get-tuple-element.111), custom_call_target="InvertDiagBlocksLowerTriangular" | custom-call | tf_op jit(solution)/shard_map/jit(_cho_solve)/triangular_solve | solution.py:23
  463.1 13.4 %collective-permute-done.8 = f32[256,640]{1,0:T(8,128)S(1)} collective-permute-done((f32[256,640]{1,0:T(8,128)}, f32[256,640]{1,0:T(8,128)S(1)}, u32[]{:S(2)}, u32[]{:S(2)}) %collective-permute-start.8) | collective-permute-done | bytes 655392 | tf_op jit(solution)/shard_map/ppermute | solution.py:15
  483.9 11.7 %cholesky.636 = f32[128,128]{1,0:T(8,128)S(1)} custom-call(f32[128,128]{1,0:T(8,128)S(1)} %cholesky.817), custom_call_target="Cholesky" | custom-call | tf_op jit(solution)/shard_map/jit(cholesky)/cholesky | solution.py:28
  495.7 9.8 %custom-call.48 = f32[1,128,128]{1,2,0:T(8,128)S(1)} custom-call(f32[1,128,128]{2,1,0:T(8,128)S(1)} %get-tuple-element.271), custom_call_target="InvertDiagBlocksLowerTriangular" | custom-call | tf_op jit(solution)/shard_map/jit(cholesky)/cholesky | solution.py:28
  506.0 11.9 %cholesky.653 = f32[128,128]{1,0:T(8,128)S(1)} custom-call(f32[128,128]{1,0:T(8,128)S(1)} %convolution_subtract_fusion.23), custom_call_target="Cholesky" | custom-call | tf_op jit(solution)/shard_map/jit(cholesky)/cholesky | solution.py:28
  525.0 19.7 %custom-call.49 = f32[2,128,128]{1,2,0:T(8,128)S(1)} custom-call(f32[2,128,128]{2,1,0:T(8,128)S(1)} %get-tuple-element.112), custom_call_target="InvertDiagBlocksLowerTriangular" | custom-call | tf_op jit(solution)/shard_map/jit(_cho_solve)/triangular_solve | solution.py:23
  550.0 5.1 collective-permute-start.10
  556.4 25.5 %collective-permute-done.10 = f32[256,640]{1,0:T(8,128)} collective-permute-done((f32[256,640]{1,0:T(8,128)}, f32[256,640]{1,0:T(8,128)}, u32[]{:S(2)}, u32[]{:S(2)}) %collective-permute-start.10) | collective-permute-done | bytes 655392 | tf_op jit(solution)/shard_map/ppermute | solution.py:15
  588.2 11.7 %cholesky.670 = f32[128,128]{1,0:T(8,128)S(1)} custom-call(f32[128,128]{1,0:T(8,128)S(1)} %cholesky.820), custom_call_target="Cholesky" | custom-call | tf_op jit(solution)/shard_map/jit(cholesky)/cholesky | solution.py:28
  600.0 9.8 %custom-call.50 = f32[1,128,128]{1,2,0:T(8,128)S(1)} custom-call(f32[1,128,128]{2,1,0:T(8,128)S(1)} %get-tuple-element.267), custom_call_target="InvertDiagBlocksLowerTriangular" | custom-call | tf_op jit(solution)/shard_map/jit(cholesky)/cholesky | solution.py:28
  610.3 11.7 %cholesky.687 = f32[128,128]{1,0:T(8,128)S(1)} custom-call(f32[128,128]{1,0:T(8,128)S(1)} %convolution_subtract_fusion.22), custom_call_target="Cholesky" | custom-call | tf_op jit(solution)/shard_map/jit(cholesky)/cholesky | solution.py:28
  628.9 19.7 %custom-call.51 = f32[2,128,128]{1,2,0:T(8,128)S(1)} custom-call(f32[2,128,128]{2,1,0:T(8,128)S(1)} %get-tuple-element.113), custom_call_target="InvertDiagBlocksLowerTriangular" | custom-call | tf_op jit(solution)/shard_map/jit(_cho_solve)/triangular_solve | solution.py:23
  652.6 4.7 collective-permute-start.12
  658.6 10.5 %collective-permute-done.12 = f32[256,640]{1,0:T(8,128)} collective-permute-done((f32[256,640]{1,0:T(8,128)S(1)}, f32[256,640]{1,0:T(8,128)}, u32[]{:S(2)}, u32[]{:S(2)}) %collective-permute-start.12) | collective-permute-done | bytes 655392 | tf_op jit(solution)/shard_map/ppermute | solution.py:15
  677.2 11.7 %cholesky.704 = f32[128,128]{1,0:T(8,128)S(1)} custom-call(f32[128,128]{1,0:T(8,128)S(1)} %cholesky.823), custom_call_target="Cholesky" | custom-call | tf_op jit(solution)/shard_map/jit(cholesky)/cholesky | solution.py:28
  688.9 9.8 %custom-call.52 = f32[1,128,128]{1,2,0:T(8,128)S(1)} custom-call(f32[1,128,128]{2,1,0:T(8,128)S(1)} %get-tuple-element.263), custom_call_target="InvertDiagBlocksLowerTriangular" | custom-call | tf_op jit(solution)/shard_map/jit(cholesky)/cholesky | solution.py:28
  699.2 11.7 %cholesky.721 = f32[128,128]{1,0:T(8,128)S(1)} custom-call(f32[128,128]{1,0:T(8,128)S(1)} %convolution_subtract_fusion.21), custom_call_target="Cholesky" | custom-call | tf_op jit(solution)/shard_map/jit(cholesky)/cholesky | solution.py:28
  714.0 4.3 while.30
  718.2 19.7 %custom-call.53 = f32[2,128,128]{1,2,0:T(8,128)S(1)} custom-call(f32[2,128,128]{2,1,0:T(8,128)S(1)} %get-tuple-element.114), custom_call_target="InvertDiagBlocksLowerTriangular" | custom-call | tf_op jit(solution)/shard_map/jit(_cho_solve)/triangular_solve | solution.py:23
  741.9 8.1 collective-permute-start.14
  751.3 9.7 %collective-permute-done.14 = f32[256,640]{1,0:T(8,128)} collective-permute-done((f32[256,640]{1,0:T(8,128)S(1)}, f32[256,640]{1,0:T(8,128)}, u32[]{:S(2)}, u32[]{:S(2)}) %collective-permute-start.14) | collective-permute-done | bytes 655392 | tf_op jit(solution)/shard_map/ppermute | solution.py:15
  763.6 18.6 %collective-permute-done.15 = f32[256,640]{1,0:T(8,128)} collective-permute-done((f32[256,640]{1,0:T(8,128)S(1)}, f32[256,640]{1,0:T(8,128)}, u32[]{:S(2)}, u32[]{:S(2)}) %collective-permute-start.15) | collective-permute-done | bytes 655392 | tf_op jit(solution)/shard_map/ppermute | solution.py:15
  785.6 11.7 %cholesky.738 = f32[128,128]{1,0:T(8,128)S(1)} custom-call(f32[128,128]{1,0:T(8,128)S(1)} %cholesky.826), custom_call_target="Cholesky" | custom-call | tf_op jit(solution)/shard_map/jit(cholesky)/cholesky | solution.py:28
  797.3 9.8 %custom-call.54 = f32[1,128,128]{1,2,0:T(8,128)S(1)} custom-call(f32[1,128,128]{2,1,0:T(8,128)S(1)} %get-tuple-element.259), custom_call_target="InvertDiagBlocksLowerTriangular" | custom-call | tf_op jit(solution)/shard_map/jit(cholesky)/cholesky | solution.py:28
  807.6 11.7 %cholesky.755 = f32[128,128]{1,0:T(8,128)S(1)} custom-call(f32[128,128]{1,0:T(8,128)S(1)} %convolution_subtract_fusion.20), custom_call_target="Cholesky" | custom-call | tf_op jit(solution)/shard_map/jit(cholesky)/cholesky | solution.py:28
  822.6 4.3 while.31
  826.9 19.7 %custom-call.55 = f32[2,128,128]{1,2,0:T(8,128)S(1)} custom-call(f32[2,128,128]{2,1,0:T(8,128)S(1)} %get-tuple-element.115), custom_call_target="InvertDiagBlocksLowerTriangular" | custom-call | tf_op jit(solution)/shard_map/jit(_cho_solve)/triangular_solve | solution.py:23
  852.0 8.0 collective-permute-start.16
  859.9 10.6 %collective-permute-done.17 = f32[256,640]{1,0:T(8,128)S(1)} collective-permute-done((f32[256,640]{1,0:T(8,128)S(1)}, f32[256,640]{1,0:T(8,128)S(1)}, u32[]{:S(2)}, u32[]{:S(2)}) %collective-permute-start.17) | collective-permute-done | bytes 655392 | tf_op jit(solution)/shard_map/ppermute | solution.py:15
  872.6 11.7 %cholesky.772 = f32[128,128]{1,0:T(8,128)S(1)} custom-call(f32[128,128]{1,0:T(8,128)S(1)} %cholesky.829), custom_call_target="Cholesky" | custom-call | tf_op jit(solution)/shard_map/jit(cholesky)/cholesky | solution.py:107
  884.4 9.8 %custom-call.56 = f32[1,128,128]{1,2,0:T(8,128)S(1)} custom-call(f32[1,128,128]{2,1,0:T(8,128)S(1)} %get-tuple-element.255), custom_call_target="InvertDiagBlocksLowerTriangular" | custom-call | tf_op jit(solution)/shard_map/jit(cholesky)/cholesky | solution.py:107
  894.7 11.7 %cholesky.789 = f32[128,128]{1,0:T(8,128)S(1)} custom-call(f32[128,128]{1,0:T(8,128)S(1)} %convolution_subtract_fusion.19), custom_call_target="Cholesky" | custom-call | tf_op jit(solution)/shard_map/jit(cholesky)/cholesky | solution.py:107
  913.0 19.7 %custom-call.20 = f32[2,128,128]{1,2,0:T(8,128)S(1)} custom-call(f32[2,128,128]{2,1,0:T(8,128)S(1)} %get-tuple-element.58), custom_call_target="InvertDiagBlocksLowerTriangular" | custom-call | tf_op jit(solution)/shard_map/jit(_cho_solve)/triangular_solve | solution.py:23
  938.4 22.8 %collective-permute-done.18 = f32[256,128]{1,0:T(8,128)S(1)} collective-permute-done((f32[256,128]{1,0:T(8,128)S(1)}, f32[256,128]{1,0:T(8,128)S(1)}, u32[]{:S(2)}, u32[]{:S(2)}) %collective-permute-start.18) | collective-permute-done | bytes 131104 | tf_op jit(solution)/shard_map/ppermute | solution.py:15
  (472 shorter events, 212.6 us)
Async XLA Ops:
  1.1 12.7 %collective-permute-start = (f32[256,256]{1,0:T(8,128)S(1)}, f32[256,256]{1,0:T(8,128)S(1)}, u32[]{:S(2)}, u32[]{:S(2)}) collective-permute-start(f32[256,256]{1,0:T(8,128)S(1)} %get-tuple-element.247), channel_id=1, source_target_pairs={{1,0},{2,1},{3,2},{4,3},{5,4},{6,5},{7,6},{8,7},{9,8},{10,9},{11,1... | collective-permute-start | bytes 786440 | tf_op jit(solution)/shard_map/ppermute | solution.py:15
  7.7 0.7 copy-start.31
  11.6 2.1 copy-start.23
  13.8 0.7 copy-start.30
  77.7 1.0 copy-start.14
  80.8 18.5 %collective-permute-start.1 = (f32[256,640]{0,1:T(8,128)}, f32[256,640]{0,1:T(8,128)S(1)}, u32[]{:S(2)}, u32[]{:S(2)}) collective-permute-start(f32[256,640]{0,1:T(8,128)} %fusion.4), channel_id=1, source_target_pairs={{1,0},{2,1},{3,2},{4,3},{5,4},{6,5},{7,6},{8,7},{9,8},{10,9},{11,1... | collective-permute-start | bytes 1966088 | tf_op jit(solution)/shard_map/ppermute | solution.py:15
  83.5 0.9 slice-start.7
  136.7 36.4 %copy-start.24 = (f32[1,256,128]{1,2,0:T(8,128)S(1)}, f32[1,256,128]{1,2,0:T(8,128)}, u32[]{:S(2)}) copy-start(f32[1,256,128]{1,2,0:T(8,128)} %copy.65) | copy-start | bytes 393220
  173.1 1.0 copy-start.15
  174.0 0.9 copy-start.25
  178.8 19.3 %collective-permute-start.2 = (f32[256,640]{1,0:T(8,128)}, f32[256,640]{1,0:T(8,128)}, u32[]{:S(2)}, u32[]{:S(2)}) collective-permute-start(f32[256,640]{1,0:T(8,128)} %pad_maximum_fusion.2), channel_id=1, source_target_pairs={{0,1},{1,2},{2,3},{3,4},{4,5},{5,6},{6,7},{7,8},{8,9},{9,10},{10,1... | collective-permute-start | bytes 1966088 | tf_op jit(solution)/shard_map/ppermute | solution.py:15
  180.8 20.0 %collective-permute-start.3 = (f32[256,640]{1,0:T(8,128)}, f32[256,640]{1,0:T(8,128)}, u32[]{:S(2)}, u32[]{:S(2)}) collective-permute-start(f32[256,640]{1,0:T(8,128)} %pad_maximum_fusion.2), channel_id=1, source_target_pairs={{1,0},{2,1},{3,2},{4,3},{5,4},{6,5},{7,6},{8,7},{9,8},{10,9},{11,1... | collective-permute-start | bytes 1966088 | tf_op jit(solution)/shard_map/ppermute | solution.py:15
  202.7 0.9 copy-start
  241.1 24.0 %copy-start.16 = (f32[256,128]{1,0:T(8,128)S(1)}, f32[256,128]{1,0:T(8,128)}, u32[]{:S(2)}) copy-start(f32[256,128]{1,0:T(8,128)} %slice.457) | copy-start | bytes 393220
  265.1 0.9 slice-start
  269.9 26.7 %collective-permute-start.4 = (f32[256,640]{1,0:T(8,128)}, f32[256,640]{1,0:T(8,128)S(1)}, u32[]{:S(2)}, u32[]{:S(2)}) collective-permute-start(f32[256,640]{1,0:T(8,128)} %pad_maximum_fusion.4), channel_id=1, source_target_pairs={{0,2},{1,3},{2,4},{3,5},{4,6},{5,7},{6,8},{7,9},{8,10},{9,11},{10,... | collective-permute-start | bytes 1966088 | tf_op jit(solution)/shard_map/ppermute | solution.py:15
  275.1 29.6 %collective-permute-start.5 = (f32[256,640]{1,0:T(8,128)}, f32[256,640]{1,0:T(8,128)}, u32[]{:S(2)}, u32[]{:S(2)}) collective-permute-start(f32[256,640]{1,0:T(8,128)} %pad_maximum_fusion.4), channel_id=1, source_target_pairs={{2,0},{3,1},{4,2},{5,3},{6,4},{7,5},{8,6},{9,7},{10,8},{11,9},{12,... | collective-permute-start | bytes 1966088 | tf_op jit(solution)/shard_map/ppermute | solution.py:15
  297.4 7.2 copy-start.1
  306.6 0.9 copy-start.2
  344.8 24.0 %copy-start.17 = (f32[256,128]{1,0:T(8,128)S(1)}, f32[256,128]{1,0:T(8,128)}, u32[]{:S(2)}) copy-start(f32[256,128]{1,0:T(8,128)} %slice.463) | copy-start | bytes 393220
  368.7 1.3 copy-start.26
  368.7 1.0 slice-start.1
  370.5 0.9 copy-start.27
  374.1 11.2 %collective-permute-start.6 = (f32[256,640]{1,0:T(8,128)}, f32[256,640]{1,0:T(8,128)}, u32[]{:S(2)}, u32[]{:S(2)}) collective-permute-start(f32[256,640]{1,0:T(8,128)} %pad_maximum_fusion.6), channel_id=1, source_target_pairs={{0,4},{1,5},{2,6},{3,7},{4,8},{5,9},{6,10},{7,11},{8,12},{9,13},{1... | collective-permute-start | bytes 1966088 | tf_op jit(solution)/shard_map/ppermute | solution.py:15
  377.4 12.2 %collective-permute-start.7 = (f32[256,640]{1,0:T(8,128)}, f32[256,640]{1,0:T(8,128)}, u32[]{:S(2)}, u32[]{:S(2)}) collective-permute-start(f32[256,640]{1,0:T(8,128)} %pad_maximum_fusion.6), channel_id=1, source_target_pairs={{4,0},{5,1},{6,2},{7,3},{8,4},{9,5},{10,6},{11,7},{12,8},{13,9},{1... | collective-permute-start | bytes 1966088 | tf_op jit(solution)/shard_map/ppermute | solution.py:15
  387.1 2.5 copy-start.3
  391.5 0.9 copy-start.4
  429.7 23.6 %copy-start.18 = (f32[256,128]{1,0:T(8,128)S(1)}, f32[256,128]{1,0:T(8,128)}, u32[]{:S(2)}) copy-start(f32[256,128]{1,0:T(8,128)} %slice.469) | copy-start | bytes 393220
  453.3 0.9 slice-start.2
  458.1 18.4 %collective-permute-start.8 = (f32[256,640]{1,0:T(8,128)}, f32[256,640]{1,0:T(8,128)S(1)}, u32[]{:S(2)}, u32[]{:S(2)}) collective-permute-start(f32[256,640]{1,0:T(8,128)} %pad_maximum_fusion.8), channel_id=1, source_target_pairs={{0,8},{1,9},{2,10},{3,11},{4,12},{5,13},{6,14},{7,15},{8,16},{9,17... | collective-permute-start | bytes 1966088 | tf_op jit(solution)/shard_map/ppermute | solution.py:15
  461.8 18.8 %collective-permute-start.9 = (f32[256,640]{1,0:T(8,128)}, f32[256,640]{1,0:T(8,128)}, u32[]{:S(2)}, u32[]{:S(2)}) collective-permute-start(f32[256,640]{1,0:T(8,128)} %pad_maximum_fusion.8), channel_id=1, source_target_pairs={{8,0},{9,1},{10,2},{11,3},{12,4},{13,5},{14,6},{15,7},{16,8},{17,9... | collective-permute-start | bytes 1966088 | tf_op jit(solution)/shard_map/ppermute | solution.py:15
  477.4 3.2 copy-start.5
  482.5 0.9 copy-start.6
  520.7 24.0 %copy-start.19 = (f32[256,128]{1,0:T(8,128)S(1)}, f32[256,128]{1,0:T(8,128)}, u32[]{:S(2)}) copy-start(f32[256,128]{1,0:T(8,128)} %slice.475) | copy-start | bytes 393220
  544.7 1.3 copy-start.28
  544.7 1.0 slice-start.3
  546.4 0.9 copy-start.29
  550.0 31.9 %collective-permute-start.10 = (f32[256,640]{1,0:T(8,128)}, f32[256,640]{1,0:T(8,128)}, u32[]{:S(2)}, u32[]{:S(2)}) collective-permute-start(f32[256,640]{1,0:T(8,128)} %pad_maximum_fusion.10), channel_id=1, source_target_pairs={{0,16},{1,17},{2,18},{3,19},{4,20},{5,21},{6,22},{7,23},{8,24},{9,... | collective-permute-start | bytes 1966088 | tf_op jit(solution)/shard_map/ppermute | solution.py:15
  555.1 29.4 %collective-permute-start.11 = (f32[256,640]{1,0:T(8,128)}, f32[256,640]{1,0:T(8,128)}, u32[]{:S(2)}, u32[]{:S(2)}) collective-permute-start(f32[256,640]{1,0:T(8,128)} %pad_maximum_fusion.10), channel_id=1, source_target_pairs={{16,0},{17,1},{18,2},{19,3},{20,4},{21,5},{22,6},{23,7},{24,8},{25... | collective-permute-start | bytes 1966088 | tf_op jit(solution)/shard_map/ppermute | solution.py:15
  583.8 1.1 copy-start.7
  586.8 0.9 copy-start.8
  625.1 23.6 %copy-start.20 = (f32[256,128]{1,0:T(8,128)S(1)}, f32[256,128]{1,0:T(8,128)}, u32[]{:S(2)}) copy-start(f32[256,128]{1,0:T(8,128)} %slice.481) | copy-start | bytes 393220
  648.6 0.9 slice-start.4
  652.6 16.5 %collective-permute-start.12 = (f32[256,640]{1,0:T(8,128)S(1)}, f32[256,640]{1,0:T(8,128)}, u32[]{:S(2)}, u32[]{:S(2)}) collective-permute-start(f32[256,640]{1,0:T(8,128)S(1)} %pad_maximum_fusion.12), channel_id=1, source_target_pairs={{0,32},{1,33},{2,34},{3,35},{4,36},{5,37},{6,38},{7,39},{8,40},{9,... | collective-permute-start | bytes 1966088 | tf_op jit(solution)/shard_map/ppermute | solution.py:15
  657.3 16.6 %collective-permute-start.13 = (f32[256,640]{1,0:T(8,128)S(1)}, f32[256,640]{1,0:T(8,128)}, u32[]{:S(2)}, u32[]{:S(2)}) collective-permute-start(f32[256,640]{1,0:T(8,128)S(1)} %pad_maximum_fusion.12), channel_id=1, source_target_pairs={{32,0},{33,1},{34,2},{35,3},{36,4},{37,5},{38,6},{39,7},{40,8},{41... | collective-permute-start | bytes 1966088 | tf_op jit(solution)/shard_map/ppermute | solution.py:15
  671.0 2.9 copy-start.9
  675.8 0.9 copy-start.10
  714.0 24.0 %copy-start.21 = (f32[256,128]{1,0:T(8,128)S(1)}, f32[256,128]{1,0:T(8,128)}, u32[]{:S(2)}) copy-start(f32[256,128]{1,0:T(8,128)} %slice.487) | copy-start | bytes 393220
  737.9 0.9 slice-start.5
  741.9 19.1 %collective-permute-start.14 = (f32[256,640]{1,0:T(8,128)S(1)}, f32[256,640]{1,0:T(8,128)}, u32[]{:S(2)}, u32[]{:S(2)}) collective-permute-start(f32[256,640]{1,0:T(8,128)S(1)} %pad_maximum_fusion.14), channel_id=1, source_target_pairs={{0,64},{1,65},{2,66},{3,67},{4,68},{5,69},{6,70},{7,71},{8,72},{9,... | collective-permute-start | bytes 1966088 | tf_op jit(solution)/shard_map/ppermute | solution.py:15
  750.0 32.3 %collective-permute-start.15 = (f32[256,640]{1,0:T(8,128)S(1)}, f32[256,640]{1,0:T(8,128)}, u32[]{:S(2)}, u32[]{:S(2)}) collective-permute-start(f32[256,640]{1,0:T(8,128)S(1)} %pad_maximum_fusion.14), channel_id=1, source_target_pairs={{64,0},{65,1},{66,2},{67,3},{68,4},{69,5},{70,6},{71,7},{72,8},{73... | collective-permute-start | bytes 1966088 | tf_op jit(solution)/shard_map/ppermute | solution.py:15
  762.9 19.3 %copy-start.11 = (f32[256,640]{1,0:T(8,128)S(1)}, f32[256,640]{1,0:T(8,128)}, u32[]{:S(2)}) copy-start(f32[256,640]{1,0:T(8,128)} %copy-done.10) | copy-start | bytes 1966084
  784.2 0.9 copy-start.12
  822.6 24.0 %copy-start.22 = (f32[256,128]{1,0:T(8,128)S(1)}, f32[256,128]{1,0:T(8,128)}, u32[]{:S(2)}) copy-start(f32[256,128]{1,0:T(8,128)} %slice.493) | copy-start | bytes 393220
  846.6 0.9 slice-start.6
  850.5 20.1 %copy-start.13 = (f32[256,640]{1,0:T(8,128)S(1)}, f32[256,640]{1,0:T(8,128)}, u32[]{:S(2)}) copy-start(f32[256,640]{1,0:T(8,128)} %copy-done.12) | copy-start | bytes 1966084
  850.5 20.0 %collective-permute-start.17 = (f32[256,640]{1,0:T(8,128)S(1)}, f32[256,640]{1,0:T(8,128)S(1)}, u32[]{:S(2)}, u32[]{:S(2)}) collective-permute-start(f32[256,640]{1,0:T(8,128)S(1)} %pad_maximum_fusion.16), channel_id=1, source_target_pairs={{128,0},{129,1},{130,2},{131,3},{132,4},{133,5},{134,6},{135,7},{1... | collective-permute-start | bytes 1966088 | tf_op jit(solution)/shard_map/ppermute | solution.py:15
  852.0 19.6 %collective-permute-start.16 = (f32[256,640]{1,0:T(8,128)S(1)}, f32[256,640]{1,0:T(8,128)S(1)}, u32[]{:S(2)}, u32[]{:S(2)}) collective-permute-start(f32[256,640]{1,0:T(8,128)S(1)} %pad_maximum_fusion.16), channel_id=1, source_target_pairs={{0,128},{1,129},{2,130},{3,131},{4,132},{5,133},{6,134},{7,135},{8... | collective-permute-start | bytes 1966088 | tf_op jit(solution)/shard_map/ppermute | solution.py:15
  934.3 26.8 %collective-permute-start.18 = (f32[256,128]{1,0:T(8,128)S(1)}, f32[256,128]{1,0:T(8,128)S(1)}, u32[]{:S(2)}, u32[]{:S(2)}) collective-permute-start(f32[256,128]{1,0:T(8,128)S(1)} %get-tuple-element.250), channel_id=1, source_target_pairs={{0,1},{1,2},{2,3},{3,4},{4,5},{5,6},{6,7},{7,8},{8,9},{9,10},{10,1... | collective-permute-start | bytes 393224 | tf_op jit(solution)/shard_map/ppermute | solution.py:15
where the time goes:
time: 974 us; the launch traced here: 963 us
  other arithmetic  558 us (57%)
  waiting for transfers between devices  175 us (18%)
  local copies, waits for them, and re-layouts  71 us (7%)
  starting transfers between devices  67.7 us (7%)
  matrix products  61.4 us (6%)
  between operations  15.8 us (2%)
  loops' own time  13 us (1%)
    another operation x56, other arithmetic, scaled(): jnp.linalg.cholesky(diagonal)  279 us
    another operation x30, other arithmetic, solve_with(): return jax.scipy.linalg.cho_solve((factor, True), right_side)  203 us
    ppermute x19, waiting for transfers between devices, from_behind(): return lax.ppermute(array, axis, pairs)  175 us
    ppermute x19, starting transfers between devices, from_behind(): return lax.ppermute(array, axis, pairs)  67.7 us
    another operation x65, local copies, waits for them, and re-layouts, solve_with(): return jax.scipy.linalg.cho_solve((factor, True), right_side)  36.4 us
    another operation x7, other arithmetic, shards(): separator = solve_with(jnp.linalg.cholesky(system[0]), system[3])  34.6 us
    another operation x6, other arithmetic, shards(): factors = [jnp.linalg.cholesky(schur_block)]  34 us
    dot_general x18, matrix products, multiply(): jnp.dot(left_side, right_side, precision=HIGHEST, preferred_element_type=...  29.3 us
  transfers between devices with their start and end apart: 19, of which 16 were waited for; matrix products, arithmetic and copies ran while one was open for 3% of the time, Pallas kernels for 0%

commit v1 on v0

v1 whole, which is shorter than its diff:
```python
import jax
import jax.numpy as jnp
from jax import lax
from jax.experimental import pallas as pl
from jax.experimental.pallas import tpu as pltpu
from jax.sharding import PartitionSpec as P

HIGHEST = lax.Precision.HIGHEST
F32 = jnp.float32
N = 256
H = 128
RHS = 128
DEPTH = 8
DIRECT = 3
M0, C0, O0, E0, WIDE = N, 2 * N, 2 * N + RHS, 3 * N + RHS, 4 * N
PARTS = ((64, 0, H), (128, H, H), (128, M0, N + RHS), (64, O0, H), (128, O0 + H, H + RHS))


def mul(a, b):
    return jnp.dot(a, b, precision=HIGHEST, preferred_element_type=F32)


def mul_tn(a, b):
    return lax.dot_general(a, b, (((0,), (0,)), ((), ())), precision=HIGHEST, preferred_element_type=F32)


def mul_nt(a, b):
    return lax.dot_general(a, b, (((1,), (1,)), ((), ())), precision=HIGHEST, preferred_element_type=F32)


def eliminate_panel(panel, base, lane, sub):
    cols = [jnp.broadcast_to(panel[:, base + j : base + j + 1], (8, H)) for j in range(8)]
    panel = jnp.where((lane >= base) & (lane < base + 8), jnp.where(lane - base == sub, 1.0, 0.0), panel)
    for s in (0, 2, 4, 6):
        x, y = cols[0], cols[1]
        a, b, d = (jnp.broadcast_to(q[i : i + 1, :], (8, H)) for q, i in ((x, s), (y, s), (y, s + 1)))
        r = 1.0 / (a * d - b * b)
        first, pair = sub == s, (sub == s) | (sub == s + 1)
        u = jnp.where(pair, jnp.where(first, d, -b), y * b - x * d) * r
        w = jnp.where(pair, jnp.where(first, -b, a), x * b - y * a) * r
        m = 7 - s
        wide = jnp.concatenate(cols[2:] + [panel], 1)
        q0 = jnp.broadcast_to(wide[s : s + 1, :], wide.shape)
        q1 = jnp.broadcast_to(wide[s + 1 : s + 2, :], wide.shape)
        keep = jnp.where(pair, 0.0, 1.0)
        keep, u, w = (jnp.concatenate([z] * m, 1) for z in (keep, u, w))
        wide = keep * wide + (u * q0 + w * q1)
        cols = [wide[:, H * j : H * j + H] for j in range(m - 1)]
        panel = wide[:, H * (m - 1) :]
    return panel


def inverse_half(a, middle=None):
    lane = lax.broadcasted_iota(jnp.int32, (8, H), 1)
    sub = lax.broadcasted_iota(jnp.int32, (8, H), 0)
    lanes = lax.broadcasted_iota(jnp.int32, (H, H), 1)
    for k in range(H // 8):
        if k == 8 and middle is not None:
            middle()
        base = 8 * k
        panel = eliminate_panel(a[base : base + 8, :], base, lane, sub)
        m = [
            jnp.broadcast_to(a[:, base + j : base + j + 1], (H, H)) * jnp.broadcast_to(panel[j : j + 1, :], (H, H))
            for j in range(8)
        ]
        total = ((m[0] + m[1]) + (m[2] + m[3])) + ((m[4] + m[5]) + (m[6] + m[7]))
        new = jnp.where((lanes >= base) & (lanes < base + 8), 0.0, a) - total
        parts = ([new[:base, :]] if k else []) + [panel] + ([new[base + 8 :, :]] if k < H // 8 - 1 else [])
        a = jnp.concatenate(parts, 0)
    return a


def on_diagonal():
    return lax.broadcasted_iota(jnp.int32, (N, N), 0) == lax.broadcasted_iota(jnp.int32, (N, N), 1)


def diag_of(row):
    return jnp.where(on_diagonal(), jnp.broadcast_to(row, (N, N)), 0.0)


def column_from(row):
    return jnp.sum(diag_of(row), 1, keepdims=True)


def kernel(f, p, info, out, el, vb, vs, ends, inv, send_sem, recv_sem, pass_sem):
    tm, x = lax.axis_index("tm"), lax.axis_index("sub")
    me = tm * 4 + x
    core, y, z = tm % 2, (tm // 2) % 4, tm // 8
    last = 2 ** DEPTH - 1

    def place(x, core, y, z):
        return (z * 4 + y) * 2 + core, x

    def other(q):
        return q + 1 - 2 * (q % 2)

    partners = [
        place(other(x), core, y, z),
        place(3 - x, core, y, z),
        place(x, 1 - core, y, z),
        place(x, core, other(y), z),
        place(x, core, 3 - y, z),
        place(x, core, y, other(z)),
        place(x, core, y, z + 2 - 4 * ((z // 2) % 2)),
        place(x, core, y, 7 - z),
    ]
    sibling = partners[2]

    def partner(t):
        a, b = partners[0]
        for k in range(1, DEPTH):
            a, b = jnp.where(t == k + 1, partners[k][0], a), jnp.where(t == k + 1, partners[k][1], b)
        return a, b

    def role(t):
        return jnp.where(t == 0, 0, (me >> jnp.maximum(t - 1, 0)) % 2)

    def near_side(t):
        return jnp.where(role(t) == role(t + 1), 1, 0)

    barrier = pltpu.get_barrier_semaphore()
    for to in partners:
        pl.semaphore_signal(barrier, inc=1, device_id=to, device_id_type=pl.DeviceIdType.MESH)

    def piece(side, t, c, half):
        rows, col, cols = PARTS[c]
        start = half * rows if isinstance(half, int) else pl.multiple_of(half * rows, rows)
        return el.at[side, t, pl.ds(start, rows), pl.ds(col, cols)]

    def direct(t, c, half):
        return pltpu.make_async_remote_copy(
            src_ref=piece(0, t, c, half),
            dst_ref=piece(1, t, c, half),
            send_sem=send_sem.at[t, c, half],
            recv_sem=recv_sem.at[t, c, half],
            device_id=partner(t),
            device_id_type=pl.DeviceIdType.MESH,
        )

    def passed(t, c, half):
        return pltpu.make_async_remote_copy(
            src_ref=piece(1, t, c, half),
            dst_ref=piece(1, t, c, half),
            send_sem=pass_sem.at[t, c],
            recv_sem=recv_sem.at[t, c, half],
            device_id=sibling,
            device_id_type=pl.DeviceIdType.MESH,
        )

    def send(t, *parts):
        @pl.when(t <= DIRECT)
        def _():
            for c in parts:
                direct(t, c, 0).start()
                direct(t, c, 1).start()

        @pl.when((t > DIRECT) & (t <= DEPTH))
        def _():
            for c in parts:
                direct(t, c, core).start()

    def hand_on(t, *parts):
        @pl.when(t > DIRECT)
        def _():
            for c in parts:
                direct(t, c, core).wait_recv()
                passed(t, c, core).start()

    def receive(t, *parts):
        @pl.when((t > 0) & (t <= DIRECT))
        def _():
            for c in parts:
                direct(t, c, 0).wait_recv()
                direct(t, c, 1).wait_recv()

        @pl.when(t > DIRECT)
        def _():
            for c in parts:
                passed(t, c, 1 - core).wait_recv()

    zero = jnp.zeros((N, N), F32)
    is_first, is_last = me == 0, me == last
    f1 = jnp.where(is_first, zero, f[0])
    f2 = f[1]
    p1, p2 = p[0:1, :], p[1:2, :]
    p2_column = column_from(p2)
    weight = jnp.where(is_last, p2_column / (1.0 + p2_column), jnp.ones_like(p2_column))
    el[0, 0, :, :M0] = diag_of(1.0 + p1)
    el[1, 0, :, :M0] = mul_tn(f2, f2 * weight)
    el[0, 0, :, M0:C0] = -f1
    el[1, 0, :, M0:C0] = jnp.where(is_last, zero, -f2.T)
    el[0, 0, :, C0:O0] = info[0]
    tail = mul_tn(f2, info[1] / (1.0 + p2_column))
    el[1, 0, :, C0:O0] = jnp.where(is_last, tail, jnp.zeros_like(tail))
    el[0, 0, :, O0:E0] = mul_tn(f1, f1)
    el[1, 0, :, O0:E0] = diag_of(jnp.where(is_last, jnp.ones_like(p2), 1.0 + p2))
    el[0, 0, :, E0:] = jnp.zeros((N, RHS), F32)
    el[1, 0, :, E0:] = jnp.where(is_last, jnp.zeros_like(tail), info[1])
    pl.semaphore_wait(barrier, DEPTH)

    def merge(t, _):
        near = near_side(t)
        far = 1 - near
        hand_on(t, 0)
        receive(t, 0)
        x11 = inverse_half(el[0, t, :H, :H] + el[1, t, :H, :H], lambda: hand_on(t, 1))
        receive(t, 1)
        right = el[0, t, :, H:M0] + el[1, t, :, H:M0]
        a12, a22 = right[:H], right[H:]
        w = mul(x11, a12)
        y = inverse_half(a22 - mul_tn(a12, w), lambda: hand_on(t, 2))
        wy = mul(w, y)
        inv[:H, :H] = x11 + mul_nt(wy, w)
        inv[:H, H:] = -wy
        inv[H:, :H] = -mul_nt(y, w)
        inv[H:, H:] = y
        receive(t, 2)

        @pl.when(t < DEPTH)
        def _():
            hand_on(t, 3, 4)
            vb[t, near] = mul(inv[...], el[near, t, :, M0:C0])
            receive(t, 3, 4)
            g = el[near, t, :, M0:C0]
            el[0, t + 1, :, :M0] = el[near, t, :, O0:E0] - mul_tn(g, vb[t, near])
            send(t + 1, 0, 1)

        vb[t, far] = mul(inv[...], el[far, t, :, M0:C0])
        vs[t] = mul(inv[...], el[0, t, :, C0:O0] + el[1, t, :, C0:O0])

        @pl.when(t < DEPTH)
        def _():
            g = el[near, t, :, M0:C0]
            el[0, t + 1, :, M0:C0] = -mul_tn(g, vb[t, far])
            el[0, t + 1, :, C0:O0] = el[near, t, :, E0:] - mul_tn(g, vs[t])
            send(t + 1, 2)

        @pl.when(t < DEPTH - 1)
        def _():
            g = el[far, t, :, M0:C0]
            el[0, t + 1, :, O0:E0] = el[far, t, :, O0:E0] - mul_tn(g, vb[t, far])
            el[0, t + 1, :, E0:] = el[far, t, :, E0:] - mul_tn(g, vs[t])
            send(t + 1, 3, 4)

        @pl.when(t == DEPTH)
        def _():
            vb[t, near] = jnp.zeros((N, N), F32)

        return 0

    lax.fori_loop(0, DEPTH + 1, merge, 0)

    ends[...] = jnp.zeros((2, N, RHS), F32)

    def back(k, _):
        t = DEPTH - k
        o = ends[0]
        b = vs[t] - mul(vb[t, 0], o) - mul(vb[t, 1], ends[1])
        near = near_side(t - 1)
        ends[near] = b
        ends[1 - near] = o
        return 0

    lax.fori_loop(0, DEPTH, back, 0)
    b = vs[0] - mul(vb[0, 0], ends[0]) - mul(vb[0, 1], ends[1])
    out[0] = b
    end = (info[1] + mul(f2, b)) / (1.0 + p2_column)
    out[1] = jnp.where(is_last, end, ends[1])

    def finish(k, _):
        t = k + 1
        for c in range(len(PARTS)):
            if c < 3:
                used = t <= DEPTH
            else:
                used = t < DEPTH

            @pl.when(t <= DIRECT)
            def _():
                direct(t, c, 0).wait_send()
                direct(t, c, 1).wait_send()

            @pl.when((t > DIRECT) & used)
            def _():
                direct(t, c, core).wait_send()
                passed(t, c, core).wait_send()

        return 0

    lax.fori_loop(0, DEPTH, finish, 0)


VMEM = pl.BlockSpec(memory_space=pltpu.VMEM)


def shards(transition, precision, info):
    levels = DEPTH + 1
    return pl.pallas_call(
        kernel,
        out_shape=jax.ShapeDtypeStruct((2, N, RHS), F32),
        in_specs=[VMEM, VMEM, VMEM],
        out_specs=VMEM,
        scratch_shapes=[
            pltpu.VMEM((2, levels, N, WIDE), F32),
            pltpu.VMEM((levels, 2, N, N), F32),
            pltpu.VMEM((levels, N, RHS), F32),
            pltpu.VMEM((2, N, RHS), F32),
            pltpu.VMEM((N, N), F32),
            pltpu.SemaphoreType.DMA((levels, len(PARTS), 2)),
            pltpu.SemaphoreType.DMA((levels, len(PARTS), 2)),
            pltpu.SemaphoreType.DMA((levels, len(PARTS))),
        ],
        compiler_params=pltpu.CompilerParams(
            collective_id=0, has_side_effects=True, vmem_limit_bytes=48 * 1024 * 1024
        ),
        name="smooth",
    )(transition, precision, info)


def solution(mesh):
    placed = (P(("tm", "sub"), None, None), P(("tm", "sub"), None), P(("tm", "sub"), None, None))
    return jax.shard_map(
        shards, mesh=mesh, in_specs=placed, out_specs=P(("tm", "sub"), None, None), check_vma=False
    )
```

time: 974 us -> 172 us (0.18); the launches traced: 963 us -> 171 us
  other arithmetic: 558 us -> 0 us
  waiting for transfers between devices: 175 us -> 0 us
  Pallas kernels: 0 us -> 168 us
  starting transfers between devices: 67.7 us -> 0 us
  local copies, waits for them, and re-layouts: 71 us -> 3.38 us
  matrix products: 61.4 us -> 0 us
  between operations: 15.8 us -> 0.01 us
  loops' own time: 13 us -> 0 us
    another operation x102 -> x0, other arithmetic: 553 us -> none  [the longest x56 279 us: scaled(): jnp.linalg.cholesky(diagonal)]
    ppermute x19 -> x0, waiting for transfers between devices: 175 us -> none  [from_behind(): return lax.ppermute(array, axis, pairs)]
    pallas_call x0 -> x1, Pallas kernels: none -> 168 us  [shards(): pl.pallas_call(kernel, out_shape=jax.ShapeDtypeStruct((2, N, RHS), F32),...]
    ppermute x19 -> x0, starting transfers between devices: 67.7 us -> none  [from_behind(): return lax.ppermute(array, axis, pairs)]
    another operation x92 -> x0, local copies, waits for them, and re-layouts: 41 us -> none  [the longest x65 36.4 us: solve_with(): return jax.scipy.linalg.cho_solve((factor, True), right_side)]
    dot_general x20 -> x0, matrix products: 30.9 us -> none  [the longest x18 29.3 us: multiply(): jnp.dot(left_side, right_side, precision=HIGHEST, preferred_element_type=...]
    another operation x80 -> x0, matrix products: 30.5 us -> none  [the longest x60 25.8 us: solve_with(): return jax.scipy.linalg.cho_solve((factor, True), right_side)]
    another operation x10 -> x0, loops' own time: 13 us -> none  [solve_with(): return jax.scipy.linalg.cho_solve((factor, True), right_side)]
  transfers between devices with their start and end apart: 19 -> 0, of which waited for: 16 -> 0; matrix products, arithmetic and copies ran while one was open for 3% -> 0% of each run, Pallas kernels for 0% -> 0%
where the time goes in v1:
time: 172 us; the launch traced here: 171 us
  Pallas kernels  168 us (98%)
  local copies, waits for them, and re-layouts  3.38 us (2%)
    pallas_call x1, Pallas kernels, shards(): pl.pallas_call(kernel, out_shape=jax.ShapeDtypeStruct((2, N, RHS), F32),...  168 us

profile of v1, /device:TPU:1, one launch (start us, length us, event | category | flops | bytes accessed | tf_op | source)
XLA Modules:
  0.0 171.3 jit_solution(3760156748128013756)
XLA Ops:
  0.0 0.0 copy-start
  0.0 1.0 copy-done
  1.0 0.0 copy-start.1
  1.0 0.9 copy-done.1
  2.0 0.0 copy-start.2
  2.0 0.7 copy-done.2
  2.7 167.9 %smooth.1 = f32[2,256,128]{2,1,0:T(8,128)S(1)} custom-call(f32[2,256,256]{2,1,0:T(8,128)S(1)} %copy-done, f32[2,256]{1,0:T(2,128)S(1)} %copy-done.2, f32[2,256,128]{2,1,0:T(8,128)S(1)} %copy-done.1), custom_call_target="tpu_custom_call" | custom-call | tf_op jit(solution)/shard_map/smooth/pallas_call | solution.py:298
  170.6 0.7 copy.5
Async XLA Ops:
  0.0 1.0 copy-start
  1.0 0.9 copy-start.1
  2.0 0.7 copy-start.2

commit v2 on v1

--- a/solution.py
+++ b/solution.py
@@ -5,27 +5,29 @@
 from jax.experimental.pallas import tpu as pltpu
 from jax.sharding import PartitionSpec as P
 
-HIGHEST = lax.Precision.HIGHEST
+HIGHEST, HIGH = lax.Precision.HIGHEST, lax.Precision.HIGH
 F32 = jnp.float32
 N = 256
 H = 128
 RHS = 128
 DEPTH = 8
 DIRECT = 3
+COARSE = 4
+CHAIN = 7
 M0, C0, O0, E0, WIDE = N, 2 * N, 2 * N + RHS, 3 * N + RHS, 4 * N
-PARTS = ((64, 0, H), (128, H, H), (128, M0, N + RHS), (64, O0, H), (128, O0 + H, H + RHS))
-
-
-def mul(a, b):
-    return jnp.dot(a, b, precision=HIGHEST, preferred_element_type=F32)
-
-
-def mul_tn(a, b):
-    return lax.dot_general(a, b, (((0,), (0,)), ((), ())), precision=HIGHEST, preferred_element_type=F32)
-
-
-def mul_nt(a, b):
-    return lax.dot_general(a, b, (((1,), (1,)), ((), ())), precision=HIGHEST, preferred_element_type=F32)
+PARTS = ((64, 0, H), (128, H, H), (128, M0, N + RHS), (64, O0, H), (128, O0 + H, H + RHS), (128, C0, RHS))
+
+
+def mul(a, b, precision=HIGHEST):
+    return jnp.dot(a, b, precision=precision, preferred_element_type=F32)
+
+
+def mul_tn(a, b, precision=HIGHEST):
+    return lax.dot_general(a, b, (((0,), (0,)), ((), ())), precision=precision, preferred_element_type=F32)
+
+
+def mul_nt(a, b, precision=HIGHEST):
+    return lax.dot_general(a, b, (((1,), (1,)), ((), ())), precision=precision, preferred_element_type=F32)
 
 
 def eliminate_panel(panel, base, lane, sub):
@@ -82,7 +84,7 @@
     return jnp.sum(diag_of(row), 1, keepdims=True)
 
 
-def kernel(f, p, info, out, el, vb, vs, ends, inv, send_sem, recv_sem, pass_sem):
+def kernel(f, p, info, out, el, vb, vs, ends, inv, send_sem, recv_sem, pass_sem, chain_sem):
     tm, x = lax.axis_index("tm"), lax.axis_index("sub")
     me = tm * 4 + x
     core, y, z = tm % 2, (tm // 2) % 4, tm // 8
@@ -101,10 +103,15 @@
         place(x, core, other(y), z),
         place(x, core, 3 - y, z),
         place(x, core, y, other(z)),
-        place(x, core, y, z + 2 - 4 * ((z // 2) % 2)),
+        place(x, core, y, z + 3 - 2 * (z % 4)),
         place(x, core, y, 7 - z),
     ]
     sibling = partners[2]
+    buddy = partners[5]
+
+    def inner(t):
+        middle = ((z + 1) // 2) % 2
+        return jnp.where(t < CHAIN, 1, jnp.where(t == CHAIN, middle, 1 - middle)) == 1
 
     def partner(t):
         a, b = partners[0]
@@ -147,6 +154,16 @@
             device_id_type=pl.DeviceIdType.MESH,
         )
 
+    def chained(t, c, half):
+        return pltpu.make_async_remote_copy(
+            src_ref=piece(1, t, c, half),
+            dst_ref=piece(1, t, c, half),
+            send_sem=chain_sem.at[t, c],
+            recv_sem=recv_sem.at[t, c, half],
+            device_id=buddy,
+            device_id_type=pl.DeviceIdType.MESH,
+        )
+
     def send(t, *parts):
         @pl.when(t <= DIRECT)
         def _():
@@ -154,7 +171,7 @@
                 direct(t, c, 0).start()
                 direct(t, c, 1).start()
 
-        @pl.when((t > DIRECT) & (t <= DEPTH))
+        @pl.when((t > DIRECT) & inner(t))
         def _():
             for c in parts:
                 direct(t, c, core).start()
@@ -165,6 +182,10 @@
             for c in parts:
                 direct(t, c, core).wait_recv()
                 passed(t, c, core).start()
+
+                @pl.when((t >= CHAIN) & inner(t))
+                def _():
+                    chained(t, c, core).start()
 
     def receive(t, *parts):
         @pl.when((t > 0) & (t <= DIRECT))
@@ -183,107 +204,158 @@
     f1 = jnp.where(is_first, zero, f[0])
     f2 = f[1]
     p1, p2 = p[0:1, :], p[1:2, :]
-    p2_column = column_from(p2)
-    weight = jnp.where(is_last, p2_column / (1.0 + p2_column), jnp.ones_like(p2_column))
     el[0, 0, :, :M0] = diag_of(1.0 + p1)
-    el[1, 0, :, :M0] = mul_tn(f2, f2 * weight)
     el[0, 0, :, M0:C0] = -f1
-    el[1, 0, :, M0:C0] = jnp.where(is_last, zero, -f2.T)
     el[0, 0, :, C0:O0] = info[0]
-    tail = mul_tn(f2, info[1] / (1.0 + p2_column))
-    el[1, 0, :, C0:O0] = jnp.where(is_last, tail, jnp.zeros_like(tail))
     el[0, 0, :, O0:E0] = mul_tn(f1, f1)
-    el[1, 0, :, O0:E0] = diag_of(jnp.where(is_last, jnp.ones_like(p2), 1.0 + p2))
     el[0, 0, :, E0:] = jnp.zeros((N, RHS), F32)
-    el[1, 0, :, E0:] = jnp.where(is_last, jnp.zeros_like(tail), info[1])
+
+    @pl.when(jnp.logical_not(is_last))
+    def _():
+        el[1, 0, :, :M0] = mul_tn(f2, f2)
+        el[1, 0, :, M0:C0] = -f2.T
+        el[1, 0, :, C0:O0] = jnp.zeros((N, RHS), F32)
+        el[1, 0, :, O0:E0] = diag_of(1.0 + p2)
+        el[1, 0, :, E0:] = info[1]
+
+    @pl.when(is_last)
+    def _():
+        p2_column = column_from(p2)
+        el[1, 0, :, :M0] = mul_tn(f2, f2 * (p2_column / (1.0 + p2_column)))
+        el[1, 0, :, M0:C0] = zero
+        el[1, 0, :, C0:O0] = mul_tn(f2, info[1] / (1.0 + p2_column))
+        el[1, 0, :, O0:E0] = diag_of(jnp.ones_like(p2))
+        el[1, 0, :, E0:] = jnp.zeros((N, RHS), F32)
+
     pl.semaphore_wait(barrier, DEPTH)
 
     def merge(t, _):
         near = near_side(t)
         far = 1 - near
+
+        def hand_on_coupling():
+            @pl.when(t < DEPTH)
+            def _():
+                hand_on(t, 2)
+
+            @pl.when(t == DEPTH)
+            def _():
+                hand_on(t, 5)
+
         hand_on(t, 0)
         receive(t, 0)
         x11 = inverse_half(el[0, t, :H, :H] + el[1, t, :H, :H], lambda: hand_on(t, 1))
         receive(t, 1)
         right = el[0, t, :, H:M0] + el[1, t, :, H:M0]
         a12, a22 = right[:H], right[H:]
-        w = mul(x11, a12)
-        y = inverse_half(a22 - mul_tn(a12, w), lambda: hand_on(t, 2))
-        wy = mul(w, y)
-        inv[:H, :H] = x11 + mul_nt(wy, w)
-        inv[:H, H:] = -wy
-        inv[H:, :H] = -mul_nt(y, w)
-        inv[H:, H:] = y
-        receive(t, 2)
-
-        @pl.when(t < DEPTH)
-        def _():
-            hand_on(t, 3, 4)
-            vb[t, near] = mul(inv[...], el[near, t, :, M0:C0])
-            receive(t, 3, 4)
-            g = el[near, t, :, M0:C0]
-            el[0, t + 1, :, :M0] = el[near, t, :, O0:E0] - mul_tn(g, vb[t, near])
-            send(t + 1, 0, 1)
-
-        vb[t, far] = mul(inv[...], el[far, t, :, M0:C0])
-        vs[t] = mul(inv[...], el[0, t, :, C0:O0] + el[1, t, :, C0:O0])
-
-        @pl.when(t < DEPTH)
-        def _():
-            g = el[near, t, :, M0:C0]
-            el[0, t + 1, :, M0:C0] = -mul_tn(g, vb[t, far])
-            el[0, t + 1, :, C0:O0] = el[near, t, :, E0:] - mul_tn(g, vs[t])
-            send(t + 1, 2)
-
-        @pl.when(t < DEPTH - 1)
-        def _():
-            g = el[far, t, :, M0:C0]
-            el[0, t + 1, :, O0:E0] = el[far, t, :, O0:E0] - mul_tn(g, vb[t, far])
-            el[0, t + 1, :, E0:] = el[far, t, :, E0:] - mul_tn(g, vs[t])
-            send(t + 1, 3, 4)
-
-        @pl.when(t == DEPTH)
-        def _():
-            vb[t, near] = jnp.zeros((N, N), F32)
-
+        def by_level(step):
+            @pl.when(t < COARSE)
+            def _():
+                step(HIGHEST)
+
+            @pl.when(t >= COARSE)
+            def _():
+                step(HIGH)
+
+        def complement(precision):
+            w = mul(x11, a12, precision)
+            inv[:H, H:] = w
+            inv[H:, H:] = a22 - mul_tn(a12, w, precision)
+
+        by_level(complement)
+        y = inverse_half(inv[H:, H:], hand_on_coupling)
+
+        def finish_level(precision):
+            w = inv[:H, H:]
+            wy = mul(w, y, precision)
+            inv[:H, :H] = x11 + mul_nt(wy, w, precision)
+            inv[:H, H:] = -wy
+            inv[H:, :H] = -mul_nt(y, w, precision)
+            inv[H:, H:] = y
+
+            @pl.when(t < DEPTH)
+            def _():
+                receive(t, 2)
+                hand_on(t, 3, 4)
+                vb[t, near] = mul(inv[...], el[near, t, :, M0:C0], precision)
+                receive(t, 3, 4)
+                g = el[near, t, :, M0:C0]
+                el[0, t + 1, :, :M0] = el[near, t, :, O0:E0] - mul_tn(g, vb[t, near], precision)
+                send(t + 1, 0, 1)
+                vs[t] = mul(inv[...], el[0, t, :, C0:O0] + el[1, t, :, C0:O0], precision)
+                el[0, t + 1, :, C0:O0] = el[near, t, :, E0:] - mul_tn(g, vs[t], precision)
+                vb[t, far] = mul(inv[...], el[far, t, :, M0:C0], precision)
+
+            @pl.when(t == DEPTH - 1)
+            def _():
+                send(t + 1, 5)
+
+            @pl.when(t < DEPTH - 1)
+            def _():
+                g = el[near, t, :, M0:C0]
+                el[0, t + 1, :, M0:C0] = -mul_tn(g, vb[t, far], precision)
+                send(t + 1, 2)
+                g = el[far, t, :, M0:C0]
+                el[0, t + 1, :, O0:E0] = el[far, t, :, O0:E0] - mul_tn(g, vb[t, far], precision)
+                el[0, t + 1, :, E0:] = el[far, t, :, E0:] - mul_tn(g, vs[t], precision)
+                send(t + 1, 3, 4)
+
+            @pl.when(t == DEPTH)
+            def _():
+                receive(t, 5)
+                vs[t] = mul(inv[...], el[0, t, :, C0:O0] + el[1, t, :, C0:O0], precision)
+
+        by_level(finish_level)
         return 0
 
     lax.fori_loop(0, DEPTH + 1, merge, 0)
 
-    ends[...] = jnp.zeros((2, N, RHS), F32)
+    near = near_side(DEPTH - 1)
+    ends[near] = vs[DEPTH]
+    ends[1 - near] = jnp.zeros((N, RHS), F32)
 
     def back(k, _):
-        t = DEPTH - k
+        t = DEPTH - 1 - k
         o = ends[0]
-        b = vs[t] - mul(vb[t, 0], o) - mul(vb[t, 1], ends[1])
+        b = vs[t] - mul(vb[t, 0], o, HIGH) - mul(vb[t, 1], ends[1], HIGH)
         near = near_side(t - 1)
         ends[near] = b
         ends[1 - near] = o
         return 0
 
-    lax.fori_loop(0, DEPTH, back, 0)
-    b = vs[0] - mul(vb[0, 0], ends[0]) - mul(vb[0, 1], ends[1])
+    lax.fori_loop(0, DEPTH - 1, back, 0)
+    b = vs[0] - mul(vb[0, 0], ends[0], HIGH) - mul(vb[0, 1], ends[1], HIGH)
     out[0] = b
-    end = (info[1] + mul(f2, b)) / (1.0 + p2_column)
-    out[1] = jnp.where(is_last, end, ends[1])
+
+    @pl.when(jnp.logical_not(is_last))
+    def _():
+        out[1] = ends[1]
+
+    @pl.when(is_last)
+    def _():
+        out[1] = (info[1] + mul(f2, b)) / (1.0 + column_from(p2))
 
     def finish(k, _):
         t = k + 1
         for c in range(len(PARTS)):
-            if c < 3:
-                used = t <= DEPTH
-            else:
-                used = t < DEPTH
-
-            @pl.when(t <= DIRECT)
+            used = {0: t > 0, 1: t > 0, 5: t == DEPTH}.get(c, t < DEPTH)
+
+            @pl.when((t <= DIRECT) & used)
             def _():
                 direct(t, c, 0).wait_send()
                 direct(t, c, 1).wait_send()
 
             @pl.when((t > DIRECT) & used)
             def _():
+                passed(t, c, core).wait_send()
+
+            @pl.when((t > DIRECT) & used & inner(t))
+            def _():
                 direct(t, c, core).wait_send()
-                passed(t, c, core).wait_send()
+
+            @pl.when((t >= CHAIN) & used & inner(t))
+            def _():
+                chained(t, c, core).wait_send()
 
         return 0
 
@@ -309,6 +381,7 @@
             pltpu.SemaphoreType.DMA((levels, len(PARTS), 2)),
             pltpu.SemaphoreType.DMA((levels, len(PARTS), 2)),
             pltpu.SemaphoreType.DMA((levels, len(PARTS))),
+            pltpu.SemaphoreType.DMA((levels, len(PARTS))),
         ],
         compiler_params=pltpu.CompilerParams(
             collective_id=0, has_side_effects=True, vmem_limit_bytes=48 * 1024 * 1024

time: 172 us -> 161 us (0.936)
  Pallas kernels: 168 us -> 156 us
    pallas_call x1, Pallas kernels: 168 us -> 156 us  [shards(): pl.pallas_call(kernel, out_shape=jax.ShapeDtypeStruct((2, N, RHS), F32),...]
where the time goes in v2:
time: 161 us; the launch traced here: 160 us
  Pallas kernels  156 us (97%)
  local copies, waits for them, and re-layouts  3.38 us (2%)
    pallas_call x1, Pallas kernels, shards(): pl.pallas_call(kernel, out_shape=jax.ShapeDtypeStruct((2, N, RHS), F32),...  156 us
    unnamed x7, local copies, waits for them, and re-layouts  3.38 us

profile of v2, /device:TPU:1, one launch (start us, length us, event | category | flops | bytes accessed | tf_op | source)
XLA Modules:
  0.0 159.7 jit_solution(15524062016514705585)
XLA Ops:
  0.0 0.0 copy-start
  0.0 1.0 copy-done
  1.0 0.0 copy-start.1
  1.0 0.9 copy-done.1
  2.0 0.0 copy-start.2
  2.0 0.7 copy-done.2
  2.7 156.3 %smooth.1 = f32[2,256,128]{2,1,0:T(8,128)S(1)} custom-call(f32[2,256,256]{2,1,0:T(8,128)S(1)} %copy-done, f32[2,256]{1,0:T(2,128)S(1)} %copy-done.2, f32[2,256,128]{2,1,0:T(8,128)S(1)} %copy-done.1), custom_call_target="tpu_custom_call" | custom-call | tf_op jit(solution)/shard_map/smooth/pallas_call | solution.py:370
  158.9 0.7 copy.5
Async XLA Ops:
  0.0 1.0 copy-start
  1.0 0.9 copy-start.1
  2.0 0.7 copy-start.2

commit v3 on v2

--- a/solution.py
+++ b/solution.py
@@ -278,9 +278,10 @@
                 receive(t, 2)
                 hand_on(t, 3, 4)
                 vb[t, near] = mul(inv[...], el[near, t, :, M0:C0], precision)
+                g = el[near, t, :, M0:C0]
+                product = mul_tn(g, vb[t, near], precision)
                 receive(t, 3, 4)
-                g = el[near, t, :, M0:C0]
-                el[0, t + 1, :, :M0] = el[near, t, :, O0:E0] - mul_tn(g, vb[t, near], precision)
+                el[0, t + 1, :, :M0] = el[near, t, :, O0:E0] - product
                 send(t + 1, 0, 1)
                 vs[t] = mul(inv[...], el[0, t, :, C0:O0] + el[1, t, :, C0:O0], precision)
                 el[0, t + 1, :, C0:O0] = el[near, t, :, E0:] - mul_tn(g, vs[t], precision)

time: 161 us -> 158 us (0.981)
  Pallas kernels: 156 us -> 154 us
    pallas_call x1, Pallas kernels: 156 us -> 154 us  [shards(): pl.pallas_call(kernel, out_shape=jax.ShapeDtypeStruct((2, N, RHS), F32),...]
where the time goes in v3:
time: 158 us; the launch traced here: 157 us
  Pallas kernels  154 us (97%)
  local copies, waits for them, and re-layouts  3.38 us (2%)
    pallas_call x1, Pallas kernels, shards(): pl.pallas_call(kernel, out_shape=jax.ShapeDtypeStruct((2, N, RHS), F32),...  154 us
    unnamed x7, local copies, waits for them, and re-layouts  3.38 us

profile of v3, /device:TPU:1, one launch (start us, length us, event | category | flops | bytes accessed | tf_op | source)
XLA Modules:
  0.0 156.9 jit_solution(5842385611929103562)
XLA Ops:
  0.0 0.0 copy-start
  0.0 1.0 copy-done
  1.0 0.0 copy-start.1
  1.0 0.9 copy-done.1
  2.0 0.0 copy-start.2
  2.0 0.7 copy-done.2
  2.7 153.5 %smooth.1 = f32[2,256,128]{2,1,0:T(8,128)S(1)} custom-call(f32[2,256,256]{2,1,0:T(8,128)S(1)} %copy-done, f32[2,256]{1,0:T(2,128)S(1)} %copy-done.2, f32[2,256,128]{2,1,0:T(8,128)S(1)} %copy-done.1), custom_call_target="tpu_custom_call" | custom-call | tf_op jit(solution)/shard_map/smooth/pallas_call | solution.py:371
  156.2 0.7 copy.5
Async XLA Ops:
  0.0 1.0 copy-start
  1.0 0.9 copy-start.1
  2.0 0.7 copy-start.2

commit v4 on v3

--- a/solution.py
+++ b/solution.py
@@ -279,9 +279,11 @@
                 hand_on(t, 3, 4)
                 vb[t, near] = mul(inv[...], el[near, t, :, M0:C0], precision)
                 g = el[near, t, :, M0:C0]
-                product = mul_tn(g, vb[t, near], precision)
+                upper = mul_tn(g[:, :H], vb[t, near], precision)
+                lower = mul_tn(g[:, H:], vb[t, near, :, H:], precision)
                 receive(t, 3, 4)
-                el[0, t + 1, :, :M0] = el[near, t, :, O0:E0] - product
+                el[0, t + 1, :H, :M0] = el[near, t, :H, O0:E0] - upper
+                el[0, t + 1, H:, H:M0] = el[near, t, H:, O0 + H : E0] - lower
                 send(t + 1, 0, 1)
                 vs[t] = mul(inv[...], el[0, t, :, C0:O0] + el[1, t, :, C0:O0], precision)
                 el[0, t + 1, :, C0:O0] = el[near, t, :, E0:] - mul_tn(g, vs[t], precision)

time: 158 us -> 158 us (level)
  no operation moved by 1% of the time
where the time goes in v4:
time: 158 us; the launch traced here: 157 us
  Pallas kernels  153 us (97%)
  local copies, waits for them, and re-layouts  3.38 us (2%)
    pallas_call x1, Pallas kernels, shards(): pl.pallas_call(kernel, out_shape=jax.ShapeDtypeStruct((2, N, RHS), F32),...  153 us
    unnamed x7, local copies, waits for them, and re-layouts  3.38 us

profile of v4, /device:TPU:1, one launch (start us, length us, event | category | flops | bytes accessed | tf_op | source)
XLA Modules:
  0.0 156.8 jit_solution(7214225357539067575)
XLA Ops:
  0.0 0.0 copy-start
  0.0 1.0 copy-done
  1.0 0.0 copy-start.1
  1.0 0.9 copy-done.1
  2.0 0.0 copy-start.2
  2.0 0.7 copy-done.2
  2.7 153.5 %smooth.1 = f32[2,256,128]{2,1,0:T(8,128)S(1)} custom-call(f32[2,256,256]{2,1,0:T(8,128)S(1)} %copy-done, f32[2,256]{1,0:T(2,128)S(1)} %copy-done.2, f32[2,256,128]{2,1,0:T(8,128)S(1)} %copy-done.1), custom_call_target="tpu_custom_call" | custom-call | tf_op jit(solution)/shard_map/smooth/pallas_call | solution.py:373
  156.1 0.7 copy.5
Async XLA Ops:
  0.0 1.0 copy-start
  1.0 0.9 copy-start.1
  2.0 0.7 copy-start.2
